TPU v7x, 32 devices: a whole 2x2x4 slice. The times are simulated.
32 devices in a mesh: dp: 4 (over y, x), expert: 8 (over z, core).
Axes of the slice: x: 2, y: 2, z: 4, core: 2. Of those that a mesh axis runs over, the one named last changes fastest.
Arguments:
- output_grad: bfloat16 [6144, 2048], P(('dp', 'expert')), may hold values from -3 to 3
- routes: int32 [6144, 2], P(('dp', 'expert')), may hold values from 0 to 7, all different within a row; in each aligned block of 192 rows (0 to 191, 192 to 383, ...) at most 72 rows name the same one
- combine_weights: bfloat16 [6144, 2], P(('dp', 'expert')), may hold values from 0.049804688 to 0.5
- saved_hidden: bfloat16 [18432, 768], P(('dp', 'expert')), may hold values from -0.796875 to 0.796875
- down_weight: bfloat16 [8, 768, 2048], P('expert', 'dp'), may hold values from -0.21875 to 0.21875
Outputs:
- hidden_grad: bfloat16 [18432, 768], P(('dp', 'expert'))
- weight_grad: float32 [8, 768, 2048], P('expert', 'dp')
- route_grad: float32 [6144, 2], P(('dp', 'expert'))
Inputs may be any that keep to these rules, and one draw needn't show every extreme that they name: Each token names 2 different experts; among the 192 rows of one device no expert is named by more than 72 routes.
All inputs are finite; a program needn't handle non-finite values.
Results may differ from a plain program's by a relative error of at most 0.008.
Values may be sent and summed in bfloat16 or wider, within the bound.
A program may use at most 64 MiB of HBM per device.

v0:
```python
import jax
import jax.numpy as jnp
from jax import lax
from jax.sharding import PartitionSpec as P


def route_slots(routes, experts, capacity):
    flat_ids = routes.reshape(-1)
    place = jnp.arange(flat_ids.shape[0], dtype=jnp.int32)
    same = flat_ids[:, None] == flat_ids[None, :]
    rank = jnp.sum((same & (place[None, :] < place[:, None])).astype(jnp.int32), axis=1)
    return flat_ids * capacity + rank


def per_device(output_grad, routes, combine_weights, saved_hidden, down_weight):
    experts = lax.axis_size("expert")
    slot_count = saved_hidden.shape[0]
    capacity = slot_count // experts
    features = output_grad.shape[1]
    route_total = routes.shape[0] * routes.shape[1]
    target = route_slots(routes, experts, capacity)
    source = (
        jnp.full((slot_count,), route_total, jnp.int32)
        .at[target]
        .set(jnp.arange(route_total, dtype=jnp.int32))
    )
    is_live = source < route_total
    safe_index = jnp.where(is_live, source, 0)
    send_rows = jnp.where(
        is_live[:, None], output_grad[safe_index // routes.shape[1]], jnp.zeros((), jnp.bfloat16)
    )
    send_weights = jnp.where(
        is_live, combine_weights.reshape(-1)[safe_index], jnp.zeros((), jnp.bfloat16)
    )
    recv_rows, recv_weights = (
        lax.all_to_all(
            send_rows.reshape(experts, capacity, features),
            "expert",
            split_axis=0,
            concat_axis=0,
            tiled=True,
        ),
        lax.all_to_all(
            send_weights.reshape(experts, capacity),
            "expert",
            split_axis=0,
            concat_axis=0,
            tiled=True,
        ),
    )
    grad_rows = recv_rows.reshape(slot_count, features)
    slot_weights = recv_weights.reshape(slot_count).astype(jnp.float32)
    weighted = (slot_weights[:, None] * grad_rows.astype(jnp.float32)).astype(jnp.bfloat16)
    weight_shard = down_weight[0]
    contract = (((1,), (1,)), ((), ()))
    full_weight = lax.all_gather(weight_shard, "dp", axis=0, tiled=True)
    unscaled = lax.dot_general(grad_rows, full_weight, contract, preferred_element_type=jnp.float32)
    route_terms = jnp.sum(saved_hidden.astype(jnp.float32) * unscaled, axis=1)
    hidden_grad = (slot_weights[:, None] * unscaled).astype(jnp.bfloat16)
    grad_part = lax.psum_scatter(
        lax.dot_general(
            saved_hidden, weighted, (((0,), (0,)), ((), ())), preferred_element_type=jnp.float32
        ).astype(jnp.bfloat16),
        "dp",
        scatter_dimension=0,
        tiled=True,
    ).astype(jnp.float32)
    returned = lax.all_to_all(
        route_terms.reshape(experts, capacity), "expert", split_axis=0, concat_axis=0, tiled=True
    )
    route_grad = returned.reshape(-1)[target].reshape(routes.shape)
    return (hidden_grad, grad_part[None], route_grad)


def solution(mesh):
    return jax.shard_map(
        per_device,
        mesh=mesh,
        in_specs=(
            P(("dp", "expert"), None),
            P(("dp", "expert"), None),
            P(("dp", "expert"), None),
            P(("dp", "expert"), None),
            P("expert", "dp", None),
        ),
        out_specs=(P(("dp", "expert"), None), P("expert", "dp", None), P(("dp", "expert"), None)),
        check_vma=False,
    )
```

profile of v0, /device:TPU:0, one launch (start us, length us, event | category | flops | bytes accessed | tf_op | source)
XLA Modules:
  0.0 155.5 jit_solution(9721528789717610883)
XLA Ops:
  7.2 0.0 copy-start
  7.2 0.9 copy.21
  8.1 0.7 broadcast_multiply_fusion
  8.7 0.1 eq.15
  8.9 0.2 convert_reduce_fusion
  9.1 0.1 copy.20
  9.2 0.1 mul.37
  9.4 2.9 %scatter_custom_fusion = s32[576]{0:T(1024)S(1)} fusion(s32[384]{0:T(512)S(1)} %fusion.9, s32[384]{0:T(512)S(1)} %iota.10, s32[]{:T(128)} %constant.9.clone.1), kind=kCustom, calls=%fused_computation.32 | custom fusion | bytes 2308 | tf_op jit(solution)/shard_map/scatter | solution.py:25
  12.4 0.8 copy.22
  13.2 0.2 reshape.75
  13.4 3.9 %gather_fusion = bf16[576]{0:T(1024)(128)(2,1)S(1)} fusion(bf16[384]{0:T(512)(128)(2,1)S(1)} %reshape.75, s32[1024]{0:T(1024)S(1)} %pad_clamp_fusion.2), kind=kCustom, calls=%fused_computation | custom fusion | bytes 4608 | tf_op jit(solution)/shard_map/gather | solution.py:33
  17.3 0.7 all_to_all.20
  18.0 6.3 %all-to-all-start = ((bf16[8,1,72]{2,1,0:T(2,128)(2,1)}), bf16[8,1,72]{2,1,0:T(2,128)(2,1)S(1)}, u32[]{:S(2)}, u32[]{:S(2)}) async-start(bf16[8,1,72]{2,1,0:T(2,128)(2,1)} %all_to_all.20), calls=%async_computation | async-start | bytes 8192 | tf_op jit(solution)/shard_map/all_to_all | solution.py:43
  24.3 0.0 all-gather.3.cloned.1.call-start
  24.4 0.7 all-gather.3.cloned.1.call-update
  25.1 0.1 broadcast_in_dim.44
  25.2 0.0 copy-done
  25.2 3.4 %gather_fusion.1 = bf16[576,2048]{1,0:T(8,128)(2,1)S(1)} fusion(bf16[192,2048]{1,0:T(8,128)(2,1)S(1)} %copy-done, s32[1024]{0:T(1024)S(1)} %pad_clamp_fusion.1), kind=kCustom, calls=%fused_computation.1 | custom fusion | bytes 4720896 | tf_op jit(solution)/shard_map/gather | solution.py:30
  28.6 1.7 %broadcast_select_fusion = bf16[8,72,2048]{2,1,0:T(8,128)(2,1)} fusion(bf16[8,72,2048]{2,1,0:T(8,128)(2,1)S(1)} %bitcast.15, pred[8,72]{1,0:T(8,128)(4,1)S(1)} %broadcast_in_dim.44), kind=kLoop, calls=%fused_computation.10 | loop fusion | flops 1179648 | bytes 4719168 | tf_op jit(solution)/shard_map/jit(_where)/select_n | solution.py:29
  30.3 0.0 all-to-all-done
  30.3 5.1 %all-to-all-start.1 = ((bf16[8,72,2048]{2,1,0:T(8,128)(2,1)}), bf16[8,72,2048]{2,1,0:T(8,128)(2,1)S(1)}, u32[]{:S(2)}, u32[]{:S(2)}) async-start(bf16[8,72,2048]{2,1,0:T(8,128)(2,1)} %broadcast_select_fusion), calls=%async_computation.1 | async-start | bytes 4718592 | tf_op jit(solution)/shard_map/all_to_all | solution.py:36
  35.4 0.0 reduce-scatter.4.cloned.1.call-start
  35.5 0.1 reshape.79
  35.5 54.5 %all-to-all-done.1 = bf16[8,72,2048]{2,1,0:T(8,128)(2,1)S(1)} async-done(((bf16[8,72,2048]{2,1,0:T(8,128)(2,1)}), bf16[8,72,2048]{2,1,0:T(8,128)(2,1)S(1)}, u32[]{:S(2)}, u32[]{:S(2)}) %all-to-all-start.1) | async-done | bytes 2359328 | tf_op jit(solution)/shard_map/all_to_all | solution.py:36
  90.1 5.5 %fusion.2 = bf16[768,2048]{0,1:T(8,128)(2,1)} fusion(bf16[576,768]{1,0:T(8,128)(2,1)} %param.8, bf16[576,2048]{1,0:T(8,128)(2,1)S(1)} %bitcast.16, f32[576]{0:T(1024)S(1)} %reshape.79), kind=kOutput, calls=%fused_computation.8 | convolution fusion | flops 1817051136 | bytes 6392064 | tf_op jit(solution)/shard_map/dot_general | solution.py:61
  95.6 4.7 %copy.26 = bf16[768,2048]{1,0:T(8,128)(2,1)} copy(bf16[768,2048]{0,1:T(8,128)(2,1)} %fusion.2) | data formatting | bytes 6291456
  100.3 0.0 reduce-scatter.4.cloned.1.call-update
  100.3 0.0 all-gather.3.cloned.1.call-done
  100.3 5.1 %multiply_reduce_fusion = (f32[576]{0:T(1024)S(1)}, bf16[576,768]{1,0:T(8,128)(2,1)}) fusion(bf16[576,768]{1,0:T(8,128)(2,1)} %param.8, f32[576]{0:T(1024)S(1)} %reshape.79, bf16[576,2048]{1,0:T(8,128)(2,1)S(1)} %bitcast.17, bf16[1,768,2048]{2,1,0:T(8,128)(2,1)} %all-gather.3.cloned.1.call-done), kind=kOutput, calls=%fused_computation.11 | convolution fusion | flops 1814150656 | bytes 7279104 | tf_op jit(solution)/shard_map/dot_general | solution.py:57
  105.4 0.7 all_to_all.18
  106.1 3.3 %all-to-all-start.2 = ((f32[8,1,72]{2,1,0:T(1,128)}), f32[8,1,72]{2,1,0:T(1,128)S(1)}, u32[]{:S(2)}, u32[]{:S(2)}) async-start(f32[8,1,72]{2,1,0:T(1,128)} %all_to_all.18), calls=%async_computation.2 | async-start | bytes 8192 | tf_op jit(solution)/shard_map/all_to_all | solution.py:68
  109.4 5.4 %all-to-all-done.2 = f32[8,1,72]{2,1,0:T(1,128)S(1)} async-done(((f32[8,1,72]{2,1,0:T(1,128)}), f32[8,1,72]{2,1,0:T(1,128)S(1)}, u32[]{:S(2)}, u32[]{:S(2)}) %all-to-all-start.2) | async-done | bytes 2336 | tf_op jit(solution)/shard_map/all_to_all | solution.py:68
  114.8 0.5 broadcast.69
  115.3 0.7 reduce.9
  116.0 0.1 reshape.77
  116.1 1.9 %gather_fusion.2 = f32[384]{0:T(512)S(1)} fusion(f32[576]{0:T(1024)S(1)} %reshape.77, s32[1024]{0:T(1024)S(1)} %pad_clamp_fusion), kind=kCustom, calls=%fused_computation.2 | custom fusion | bytes 4608 | tf_op jit(solution)/shard_map/gather | solution.py:71
  118.0 0.1 reshape.78
  118.1 0.7 copy.25
  118.8 24.6 %reduce-scatter.4.cloned.1.call-done = bf16[192,2048]{1,0:T(8,128)(2,1)} async-done(((bf16[768,2048]{1,0:T(8,128)(2,1)}), bf16[192,2048]{1,0:T(8,128)(2,1)}) %reduce-scatter.4.cloned.1.call-update) | async-done | bytes 786448
  143.3 2.2 %copy.27 = bf16[192,2048]{0,1:T(8,128)(2,1)} copy(bf16[192,2048]{1,0:T(8,128)(2,1)} %reduce-scatter.4.cloned.1.call-done) | data formatting | bytes 1572864
  145.6 1.4 bitcast_convert_fusion
  146.9 1.7 %copy.24 = f32[1,192,2048]{2,1,0:T(8,128)} copy(f32[1,192,2048]{1,2,0:T(8,128)S(1)} %bitcast_convert_fusion) | data formatting | bytes 3145728
  (9 shorter events, 0.1 us)
Async XLA Ops:
  7.2 18.0 %copy-start = (bf16[192,2048]{1,0:T(8,128)(2,1)S(1)}, bf16[192,2048]{1,0:T(8,128)(2,1)}, u32[]{:S(2)}) copy-start(bf16[192,2048]{1,0:T(8,128)(2,1)} %param.5) | copy-start | bytes 2359300
  18.0 12.3 %all-to-all-start = ((bf16[8,1,72]{2,1,0:T(2,128)(2,1)}), bf16[8,1,72]{2,1,0:T(2,128)(2,1)S(1)}, u32[]{:S(2)}, u32[]{:S(2)}) async-start(bf16[8,1,72]{2,1,0:T(2,128)(2,1)} %all_to_all.20), calls=%async_computation | async-start | bytes 8192 | tf_op jit(solution)/shard_map/all_to_all | solution.py:43
  24.3 76.0 %all-gather.3.cloned.1.call-start = ((), (), s32[]{:S(2)}) async-start(), calls=%async_computation.4 | async-start | bytes 3932160 | tf_op jit(solution)/shard_map/all_gather | solution.py:56
  30.3 59.8 %all-to-all-start.1 = ((bf16[8,72,2048]{2,1,0:T(8,128)(2,1)}), bf16[8,72,2048]{2,1,0:T(8,128)(2,1)S(1)}, u32[]{:S(2)}, u32[]{:S(2)}) async-start(bf16[8,72,2048]{2,1,0:T(8,128)(2,1)} %broadcast_select_fusion), calls=%async_computation.1 | async-start | bytes 4718592 | tf_op jit(solution)/shard_map/all_to_all | solution.py:36
  35.4 108.0 %reduce-scatter.4.cloned.1.call-start = ((), (), s32[]{:S(2)}) async-start(), calls=%async_computation.5 | async-start | bytes 3932160
  106.1 8.7 %all-to-all-start.2 = ((f32[8,1,72]{2,1,0:T(1,128)}), f32[8,1,72]{2,1,0:T(1,128)S(1)}, u32[]{:S(2)}, u32[]{:S(2)}) async-start(f32[8,1,72]{2,1,0:T(1,128)} %all_to_all.18), calls=%async_computation.2 | async-start | bytes 8192 | tf_op jit(solution)/shard_map/all_to_all | solution.py:68
Sparse Core Ops, SparseCore 0:
  27.0 45.4 all-gather.2
  100.4 42.8 reduce-scatter.3
where the time goes:
time: 156 us; the launch traced here: 155 us
  waiting for transfers between devices  85.2 us (55%)
  local copies, waits for them, and re-layouts  25.9 us (17%)
  starting transfers between devices  14.8 us (9%)
  between operations  14.2 us (9%)
  matrix products  10.6 us (7%)
  other arithmetic  4.73 us (3%)
    all_to_all x1, waiting for transfers between devices, per_device(): lax.all_to_all(send_rows.reshape(experts, capacity, features), 'expert',...  54.5 us
    unnamed x3, waiting for transfers between devices  25.3 us
    unnamed x8, local copies, waits for them, and re-layouts  11 us
    all_to_all x1, starting transfers between devices, per_device(): lax.all_to_all(send_weights.reshape(experts, capacity), 'expert', split_a...  6.33 us
    dot_general x1, matrix products, per_device(): lax.dot_general(saved_hidden, weighted, (((0,), (0,)), ((), ())), preferr...  5.51 us
    all_to_all x1, waiting for transfers between devices, per_device(): lax.all_to_all(route_terms.reshape(experts, capacity), 'expert', split_ax...  5.4 us
    all_to_all x1, starting transfers between devices, per_device(): lax.all_to_all(send_rows.reshape(experts, capacity, features), 'expert',...  5.09 us
    dot_general x1, matrix products, per_device(): lax.dot_general(grad_rows, full_weight, contract, preferred_element_type=...  5.08 us
  transfers between devices with their start and end apart: 5, of which 3 were waited for; matrix products, arithmetic and copies ran while one was open for 16% of the time, Pallas kernels for 0%

commit v1 on v0

--- a/solution.py
+++ b/solution.py
@@ -2,6 +2,29 @@
 import jax.numpy as jnp
 from jax import lax
 from jax.sharding import PartitionSpec as P
+
+
+def split_up(x, dim, size):
+    dims = x.shape
+    blocks = x.reshape(*dims[:dim], size, dims[dim] // size, *dims[dim + 1 :])
+    return jnp.moveaxis(blocks, dim, 0)
+
+
+def joined_along(blocks, dim):
+    blocks = jnp.moveaxis(blocks, 0, dim)
+    shape = blocks.shape
+    return blocks.reshape(*shape[:dim], shape[dim] * shape[dim + 1], *shape[dim + 2 :])
+
+
+def exchange_in_pairs(array, axis, split_dim, concat_dim):
+    count, here = (lax.axis_size(axis), lax.axis_index(axis))
+    pieces = split_up(array, split_dim, count)
+    gathered = [pieces[here]]
+    for hop in range(1, count):
+        sent = pieces[here ^ hop]
+        gathered.append(lax.ppermute(sent, axis, [(i, i ^ hop) for i in range(count)]))
+    pieces = jnp.stack(gathered)[here ^ jnp.arange(count)]
+    return joined_along(pieces, concat_dim)
 
 
 def route_slots(routes, experts, capacity):
@@ -40,13 +63,7 @@
             concat_axis=0,
             tiled=True,
         ),
-        lax.all_to_all(
-            send_weights.reshape(experts, capacity),
-            "expert",
-            split_axis=0,
-            concat_axis=0,
-            tiled=True,
-        ),
+        exchange_in_pairs(send_weights.reshape(experts, capacity), "expert", 0, 0),
     )
     grad_rows = recv_rows.reshape(slot_count, features)
     slot_weights = recv_weights.reshape(slot_count).astype(jnp.float32)

time: 156 us -> 146 us (0.936)
  waiting for transfers between devices: 85.2 us -> 69.8 us
  starting transfers between devices: 14.8 us -> 21 us
    all_to_all x1, waiting for transfers between devices: 54.5 us -> 0.01 us  [per_device(): lax.all_to_all(send_rows.reshape(experts, capacity, features), 'expert',...]
    ppermute x0 -> x7, waiting for transfers between devices: none -> 39.2 us  [exchange_in_pairs(): lax.ppermute(sent, axis, [(i, i ^ hop) for i in range(count)])]
    ppermute x0 -> x7, starting transfers between devices: none -> 11.1 us  [exchange_in_pairs(): lax.ppermute(sent, axis, [(i, i ^ hop) for i in range(count)])]
    all_to_all x1 -> x0, starting transfers between devices: 6.33 us -> none  [per_device(): lax.all_to_all(send_weights.reshape(experts, capacity), 'expert', split_a...]
    unnamed x8 -> x10, local copies, waits for them, and re-layouts: 11 us -> 10.2 us
  transfers between devices with their start and end apart: 5 -> 11, of which waited for: 3 -> 4; matrix products, arithmetic and copies ran while one was open for 16% -> 24% of each run, Pallas kernels for 0% -> 0%
where the time goes in v1:
time: 146 us
  waiting for transfers between devices  69.8 us (48%)
  local copies, waits for them, and re-layouts  25.2 us (17%)
  starting transfers between devices  21 us (14%)
  between operations  14.3 us (10%)
  matrix products  10.6 us (7%)
  other arithmetic  4.74 us (3%)
    ppermute x7, waiting for transfers between devices, exchange_in_pairs(): lax.ppermute(sent, axis, [(i, i ^ hop) for i in range(count)])  39.2 us
    unnamed x3, waiting for transfers between devices  25.2 us
    ppermute x7, starting transfers between devices, exchange_in_pairs(): lax.ppermute(sent, axis, [(i, i ^ hop) for i in range(count)])  11.1 us
    unnamed x10, local copies, waits for them, and re-layouts  10.2 us
    all_to_all x1, starting transfers between devices, per_device(): lax.all_to_all(send_rows.reshape(experts, capacity, features), 'expert',...  6.46 us
    dot_general x1, matrix products, per_device(): lax.dot_general(saved_hidden, weighted, (((0,), (0,)), ((), ())), preferr...  5.52 us
    all_to_all x1, waiting for transfers between devices, per_device(): lax.all_to_all(route_terms.reshape(experts, capacity), 'expert', split_ax...  5.4 us
    dot_general x1, matrix products, per_device(): lax.dot_general(grad_rows, full_weight, contract, preferred_element_type=...  5.09 us
  transfers between devices with their start and end apart: 11, of which 4 were waited for; matrix products, arithmetic and copies ran while one was open for 24% of the time, Pallas kernels for 0%

profile of v1, /device:TPU:0, one launch (start us, length us, event | category | flops | bytes accessed | tf_op | source)
XLA Modules:
  0.0 145.7 jit_solution(3560568505112745782)
XLA Ops:
  7.2 0.0 copy-start
  7.2 0.0 all-gather.3.cloned.1.call-start
  7.2 0.7 all-gather.3.cloned.1.call-update
  7.9 0.7 broadcast_multiply_fusion
  8.6 0.8 copy.41
  9.4 0.1 copy.40
  9.5 0.1 mul.37
  9.7 0.1 eq.15
  9.8 0.2 convert_reduce_fusion
  10.1 2.9 %scatter_custom_fusion = s32[576]{0:T(1024)S(1)} fusion(s32[384]{0:T(512)S(1)} %fusion.9, s32[384]{0:T(512)S(1)} %iota.14, s32[]{:T(128)} %constant.17.clone.1), kind=kCustom, calls=%fused_computation.42 | custom fusion | bytes 2308 | tf_op jit(solution)/shard_map/scatter | solution.py:48
  13.1 0.1 broadcast_in_dim.45
  13.2 3.4 %gather_fusion.2 = bf16[576,2048]{1,0:T(8,128)(2,1)S(1)} fusion(bf16[192,2048]{1,0:T(8,128)(2,1)S(1)} %copy-done, s32[1024]{0:T(1024)S(1)} %pad_clamp_fusion.1), kind=kCustom, calls=%fused_computation.2 | custom fusion | bytes 4720896 | tf_op jit(solution)/shard_map/gather | solution.py:53
  16.6 1.7 %broadcast_select_fusion = bf16[8,72,2048]{2,1,0:T(8,128)(2,1)} fusion(bf16[8,72,2048]{2,1,0:T(8,128)(2,1)S(1)} %bitcast.53, pred[8,72]{1,0:T(8,128)(4,1)S(1)} %broadcast_in_dim.45), kind=kLoop, calls=%fused_computation.11 | loop fusion | flops 1179648 | bytes 4719168 | tf_op jit(solution)/shard_map/jit(_where)/select_n | solution.py:52
  18.3 6.5 %all-to-all-start = ((bf16[8,72,2048]{2,1,0:T(8,128)(2,1)}), bf16[8,72,2048]{2,1,0:T(8,128)(2,1)S(1)}, u32[]{:S(2)}, u32[]{:S(2)}) async-start(bf16[8,72,2048]{2,1,0:T(8,128)(2,1)} %broadcast_select_fusion), calls=%async_computation | async-start | bytes 4718592 | tf_op jit(solution)/shard_map/all_to_all | solution.py:59
  24.7 0.0 reduce-scatter.4.cloned.1.call-start
  24.8 0.1 copy.42
  25.0 0.2 reshape.85
  25.1 3.9 %gather_fusion = bf16[576]{0:T(1024)(128)(2,1)S(1)} fusion(bf16[384]{0:T(512)(128)(2,1)S(1)} %reshape.85, s32[1024]{0:T(1024)S(1)} %pad_clamp_fusion.3), kind=kCustom, calls=%fused_computation | custom fusion | bytes 4608 | tf_op jit(solution)/shard_map/gather | solution.py:56
  29.1 0.1 reshape_reshape.4
  29.2 0.5 collective-permute-start
  29.7 1.7 %collective-permute-start.1 = (bf16[1,72]{1,0:T(2,128)(2,1)S(1)}, bf16[1,72]{1,0:T(2,128)(2,1)S(1)}, u32[]{:S(2)}, u32[]{:S(2)}) collective-permute-start(bf16[1,72]{1,0:T(2,128)(2,1)S(1)} %get-tuple-element.24), channel_id=1, source_target_pairs={{0,2},{1,3},{2,0},{3,1},{4,6},{5,7},{6,4},{7,5},{8,10},{9,11},{10,... | collective-permute-start | bytes 440 | tf_op jit(solution)/shard_map/ppermute | solution.py:25
  31.4 0.0 collective-permute-start.2
  31.4 2.6 %collective-permute-start.3 = (bf16[1,72]{1,0:T(2,128)(2,1)S(1)}, bf16[1,72]{1,0:T(2,128)(2,1)S(1)}, u32[]{:S(2)}, u32[]{:S(2)}) collective-permute-start(bf16[1,72]{1,0:T(2,128)(2,1)S(1)} %get-tuple-element.22), channel_id=1, source_target_pairs={{0,4},{1,5},{2,6},{3,7},{4,0},{5,1},{6,2},{7,3},{8,12},{9,13},{10,... | collective-permute-start | bytes 440 | tf_op jit(solution)/shard_map/ppermute | solution.py:25
  34.0 0.1 collective-permute-start.4
  34.1 3.5 %collective-permute-start.5 = (bf16[1,72]{1,0:T(2,128)(2,1)S(1)}, bf16[1,72]{1,0:T(2,128)(2,1)S(1)}, u32[]{:S(2)}, u32[]{:S(2)}) collective-permute-start(bf16[1,72]{1,0:T(2,128)(2,1)S(1)} %get-tuple-element.20), channel_id=1, source_target_pairs={{0,6},{1,7},{2,4},{3,5},{4,2},{5,3},{6,0},{7,1},{8,14},{9,15},{10,... | collective-permute-start | bytes 440 | tf_op jit(solution)/shard_map/ppermute | solution.py:25
  37.7 26.3 %collective-permute-done.1 = bf16[1,72]{1,0:T(2,128)(2,1)S(1)} collective-permute-done((bf16[1,72]{1,0:T(2,128)(2,1)S(1)}, bf16[1,72]{1,0:T(2,128)(2,1)S(1)}, u32[]{:S(2)}, u32[]{:S(2)}) %collective-permute-start.1) | collective-permute-done | bytes 176 | tf_op jit(solution)/shard_map/ppermute | solution.py:25
  63.9 2.7 %collective-permute-start.6 = (bf16[1,72]{1,0:T(2,128)(2,1)S(1)}, bf16[1,72]{1,0:T(2,128)(2,1)S(1)}, u32[]{:S(2)}, u32[]{:S(2)}) collective-permute-start(bf16[1,72]{1,0:T(2,128)(2,1)S(1)} %get-tuple-element.19), channel_id=1, source_target_pairs={{0,7},{1,6},{2,5},{3,4},{4,3},{5,2},{6,1},{7,0},{8,15},{9,14},{10,... | collective-permute-start | bytes 440 | tf_op jit(solution)/shard_map/ppermute | solution.py:25
  66.6 12.9 %collective-permute-done.3 = bf16[1,72]{1,0:T(2,128)(2,1)S(1)} collective-permute-done((bf16[1,72]{1,0:T(2,128)(2,1)S(1)}, bf16[1,72]{1,0:T(2,128)(2,1)S(1)}, u32[]{:S(2)}, u32[]{:S(2)}) %collective-permute-start.3) | collective-permute-done | bytes 176 | tf_op jit(solution)/shard_map/ppermute | solution.py:25
  79.6 0.6 gather_fusion.1
  80.1 0.1 reshape.89
  80.2 5.5 %fusion.2 = bf16[768,2048]{0,1:T(8,128)(2,1)} fusion(bf16[576,768]{1,0:T(8,128)(2,1)} %param.8, bf16[576,2048]{1,0:T(8,128)(2,1)S(1)} %bitcast.54, f32[576]{0:T(1024)S(1)} %reshape.89), kind=kOutput, calls=%fused_computation.9 | convolution fusion | flops 1817051136 | bytes 6392064 | tf_op jit(solution)/shard_map/dot_general | solution.py:78
  85.8 4.7 %copy.52 = bf16[768,2048]{1,0:T(8,128)(2,1)} copy(bf16[768,2048]{0,1:T(8,128)(2,1)} %fusion.2) | data formatting | bytes 6291456
  90.5 0.0 reduce-scatter.4.cloned.1.call-update
  90.5 0.0 all-gather.3.cloned.1.call-done
  90.5 5.1 %multiply_reduce_fusion = (f32[576]{0:T(1024)S(1)}, bf16[576,768]{1,0:T(8,128)(2,1)}) fusion(bf16[576,768]{1,0:T(8,128)(2,1)} %param.8, f32[576]{0:T(1024)S(1)} %reshape.89, bf16[576,2048]{1,0:T(8,128)(2,1)S(1)} %bitcast.55, bf16[1,768,2048]{2,1,0:T(8,128)(2,1)} %all-gather.3.cloned.1.call-done), kind=kOutput, calls=%fused_computation.12 | convolution fusion | flops 1814150656 | bytes 7279104 | tf_op jit(solution)/shard_map/dot_general | solution.py:74
  95.6 0.7 all_to_all.10
  96.3 3.3 %all-to-all-start.1 = ((f32[8,1,72]{2,1,0:T(1,128)}), f32[8,1,72]{2,1,0:T(1,128)S(1)}, u32[]{:S(2)}, u32[]{:S(2)}) async-start(f32[8,1,72]{2,1,0:T(1,128)} %all_to_all.10), calls=%async_computation.1 | async-start | bytes 8192 | tf_op jit(solution)/shard_map/all_to_all | solution.py:85
  99.6 5.4 %all-to-all-done.1 = f32[8,1,72]{2,1,0:T(1,128)S(1)} async-done(((f32[8,1,72]{2,1,0:T(1,128)}), f32[8,1,72]{2,1,0:T(1,128)S(1)}, u32[]{:S(2)}, u32[]{:S(2)}) %all-to-all-start.1) | async-done | bytes 2336 | tf_op jit(solution)/shard_map/all_to_all | solution.py:85
  105.0 0.5 broadcast.105
  105.5 0.7 reduce.5
  106.2 0.1 reshape.87
  106.3 1.9 %gather_fusion.3 = f32[384]{0:T(512)S(1)} fusion(f32[576]{0:T(1024)S(1)} %reshape.87, s32[1024]{0:T(1024)S(1)} %pad_clamp_fusion), kind=kCustom, calls=%fused_computation.3 | custom fusion | bytes 4608 | tf_op jit(solution)/shard_map/gather | solution.py:88
  108.2 0.1 reshape.88
  108.3 0.7 copy.51
  109.0 24.5 %reduce-scatter.4.cloned.1.call-done = bf16[192,2048]{1,0:T(8,128)(2,1)} async-done(((bf16[768,2048]{1,0:T(8,128)(2,1)}), bf16[192,2048]{1,0:T(8,128)(2,1)}) %reduce-scatter.4.cloned.1.call-update) | async-done | bytes 786448
  133.5 2.2 %copy.53 = bf16[192,2048]{0,1:T(8,128)(2,1)} copy(bf16[192,2048]{1,0:T(8,128)(2,1)} %reduce-scatter.4.cloned.1.call-done) | data formatting | bytes 1572864
  135.7 1.4 bitcast_convert_fusion
  137.1 1.7 %copy.50 = f32[1,192,2048]{2,1,0:T(8,128)} copy(f32[1,192,2048]{1,2,0:T(8,128)S(1)} %bitcast_convert_fusion) | data formatting | bytes 3145728
  (21 shorter events, 0.2 us)
Async XLA Ops:
  7.2 6.0 %copy-start = (bf16[192,2048]{1,0:T(8,128)(2,1)S(1)}, bf16[192,2048]{1,0:T(8,128)(2,1)}, u32[]{:S(2)}) copy-start(bf16[192,2048]{1,0:T(8,128)(2,1)} %param.5) | copy-start | bytes 2359300
  7.2 83.3 %all-gather.3.cloned.1.call-start = ((), (), s32[]{:S(2)}) async-start(), calls=%async_computation.3 | async-start | bytes 3932160 | tf_op jit(solution)/shard_map/all_gather | solution.py:73
  18.3 6.5 %copy-start.1 = (bf16[192,2]{0,1:T(2,128)(2,1)S(1)}, bf16[192,2]{0,1:T(2,128)(2,1)}, u32[]{:S(2)}) copy-start(bf16[192,2]{0,1:T(2,128)(2,1)} %param.7) | copy-start | bytes 2308
  18.3 62.0 %all-to-all-start = ((bf16[8,72,2048]{2,1,0:T(8,128)(2,1)}), bf16[8,72,2048]{2,1,0:T(8,128)(2,1)S(1)}, u32[]{:S(2)}, u32[]{:S(2)}) async-start(bf16[8,72,2048]{2,1,0:T(8,128)(2,1)} %broadcast_select_fusion), calls=%async_computation | async-start | bytes 4718592 | tf_op jit(solution)/shard_map/all_to_all | solution.py:59
  24.7 108.8 %reduce-scatter.4.cloned.1.call-start = ((), (), s32[]{:S(2)}) async-start(), calls=%async_computation.4 | async-start | bytes 3932160
  29.2 4.9 %collective-permute-start = (bf16[1,72]{1,0:T(2,128)(2,1)S(1)}, bf16[1,72]{1,0:T(2,128)(2,1)S(1)}, u32[]{:S(2)}, u32[]{:S(2)}) collective-permute-start(bf16[1,72]{1,0:T(2,128)(2,1)S(1)} %get-tuple-element.25), channel_id=1, source_target_pairs={{0,1},{1,0},{2,3},{3,2},{4,5},{5,4},{6,7},{7,6},{8,9},{9,8},{10,11... | collective-permute-start | bytes 440 | tf_op jit(solution)/shard_map/ppermute | solution.py:25
  29.7 34.2 %collective-permute-start.1 = (bf16[1,72]{1,0:T(2,128)(2,1)S(1)}, bf16[1,72]{1,0:T(2,128)(2,1)S(1)}, u32[]{:S(2)}, u32[]{:S(2)}) collective-permute-start(bf16[1,72]{1,0:T(2,128)(2,1)S(1)} %get-tuple-element.24), channel_id=1, source_target_pairs={{0,2},{1,3},{2,0},{3,1},{4,6},{5,7},{6,4},{7,5},{8,10},{9,11},{10,... | collective-permute-start | bytes 440 | tf_op jit(solution)/shard_map/ppermute | solution.py:25
  31.4 35.2 %collective-permute-start.2 = (bf16[1,72]{1,0:T(2,128)(2,1)S(1)}, bf16[1,72]{1,0:T(2,128)(2,1)S(1)}, u32[]{:S(2)}, u32[]{:S(2)}) collective-permute-start(bf16[1,72]{1,0:T(2,128)(2,1)S(1)} %get-tuple-element.23), channel_id=1, source_target_pairs={{0,3},{1,2},{2,1},{3,0},{4,7},{5,6},{6,5},{7,4},{8,11},{9,10},{10,... | collective-permute-start | bytes 440 | tf_op jit(solution)/shard_map/ppermute | solution.py:25
  31.4 48.1 %collective-permute-start.3 = (bf16[1,72]{1,0:T(2,128)(2,1)S(1)}, bf16[1,72]{1,0:T(2,128)(2,1)S(1)}, u32[]{:S(2)}, u32[]{:S(2)}) collective-permute-start(bf16[1,72]{1,0:T(2,128)(2,1)S(1)} %get-tuple-element.22), channel_id=1, source_target_pairs={{0,4},{1,5},{2,6},{3,7},{4,0},{5,1},{6,2},{7,3},{8,12},{9,13},{10,... | collective-permute-start | bytes 440 | tf_op jit(solution)/shard_map/ppermute | solution.py:25
  34.0 45.6 %collective-permute-start.4 = (bf16[1,72]{1,0:T(2,128)(2,1)S(1)}, bf16[1,72]{1,0:T(2,128)(2,1)S(1)}, u32[]{:S(2)}, u32[]{:S(2)}) collective-permute-start(bf16[1,72]{1,0:T(2,128)(2,1)S(1)} %get-tuple-element.21), channel_id=1, source_target_pairs={{0,5},{1,4},{2,7},{3,6},{4,1},{5,0},{6,3},{7,2},{8,13},{9,12},{10,... | collective-permute-start | bytes 440 | tf_op jit(solution)/shard_map/ppermute | solution.py:25
  34.1 45.4 %collective-permute-start.5 = (bf16[1,72]{1,0:T(2,128)(2,1)S(1)}, bf16[1,72]{1,0:T(2,128)(2,1)S(1)}, u32[]{:S(2)}, u32[]{:S(2)}) collective-permute-start(bf16[1,72]{1,0:T(2,128)(2,1)S(1)} %get-tuple-element.20), channel_id=1, source_target_pairs={{0,6},{1,7},{2,4},{3,5},{4,2},{5,3},{6,0},{7,1},{8,14},{9,15},{10,... | collective-permute-start | bytes 440 | tf_op jit(solution)/shard_map/ppermute | solution.py:25
  63.9 15.6 %collective-permute-start.6 = (bf16[1,72]{1,0:T(2,128)(2,1)S(1)}, bf16[1,72]{1,0:T(2,128)(2,1)S(1)}, u32[]{:S(2)}, u32[]{:S(2)}) collective-permute-start(bf16[1,72]{1,0:T(2,128)(2,1)S(1)} %get-tuple-element.19), channel_id=1, source_target_pairs={{0,7},{1,6},{2,5},{3,4},{4,3},{5,2},{6,1},{7,0},{8,15},{9,14},{10,... | collective-permute-start | bytes 440 | tf_op jit(solution)/shard_map/ppermute | solution.py:25
  96.3 8.7 %all-to-all-start.1 = ((f32[8,1,72]{2,1,0:T(1,128)}), f32[8,1,72]{2,1,0:T(1,128)S(1)}, u32[]{:S(2)}, u32[]{:S(2)}) async-start(f32[8,1,72]{2,1,0:T(1,128)} %all_to_all.10), calls=%async_computation.1 | async-start | bytes 8192 | tf_op jit(solution)/shard_map/all_to_all | solution.py:85
Sparse Core Ops, SparseCore 0:
  9.9 46.6 all-gather.2
  90.6 42.8 reduce-scatter.3
